TPU v7x, 512 devices: a whole 4x4x16 slice. The times are simulated.
512 devices in a mesh: row: 16 (over x, y), col: 32 (over z, core).
Axes of the slice: x: 4, y: 4, z: 16, core: 2. Of those that a mesh axis runs over, the one named last changes fastest.
Arguments:
- species: float32 [512, 256, 2048], P(None, 'col', 'row'), may hold values from -26 to 26, as said below
- start_basis: float32 [512, 256], replicated, may hold values from -6 to 6
Outputs:
- core_fibers: float32 [256, 256, 2048], P('row', 'col')
- basis: float32 [512, 256], replicated
Inputs may be any that keep to these rules, and one draw needn't show every extreme that they name: `species`: entries of the slab.
All inputs are finite; a program needn't handle non-finite values.
Results may differ from a plain program's by a relative error of at most 0.00019.
Values sent between devices are 32-bit elements; how exact they have to be, the bound alone decides.
No kernel may reach another device: no remote copies, remote signals or barrier semaphores. Data moves between devices by JAX's collectives and lax.ppermute only.
A program may use at most 64 MiB of HBM per device.

v0:
```python
import jax
import jax.numpy as jnp
from jax import lax
from jax.sharding import PartitionSpec as P

ITERS = 2


def orthonormalize(applied):
    inner_gram = jnp.dot(
        applied.T, applied, precision=lax.Precision.HIGHEST, preferred_element_type=jnp.float32
    )
    small_lower = jnp.linalg.cholesky(inner_gram)
    return jax.scipy.linalg.solve_triangular(small_lower, applied.T, lower=True).T


def power_steps(tri_lower, start_basis):
    current = start_basis
    for sweep_number in range(ITERS):
        halfway = jnp.dot(
            tri_lower.T,
            current,
            precision=lax.Precision.HIGHEST,
            preferred_element_type=jnp.float32,
        )
        applied = jnp.dot(
            tri_lower, halfway, precision=lax.Precision.HIGHEST, preferred_element_type=jnp.float32
        )
        current = orthonormalize(applied)
    return current


def shards(species, start_basis):
    width_x, cells_z, cells_y = species.shape
    fibers = species.reshape(width_x, cells_z * cells_y)
    local_gram = jnp.dot(
        fibers, fibers.T, precision=lax.Precision.HIGHEST, preferred_element_type=jnp.float32
    )
    gram_sum = lax.psum(local_gram, ("row", "col"))
    basis = power_steps(jnp.linalg.cholesky(gram_sum), start_basis)
    core_flat = jnp.dot(
        basis.T, fibers, precision=lax.Precision.HIGHEST, preferred_element_type=jnp.float32
    )
    core_block = core_flat.reshape(basis.shape[1], cells_z, cells_y)
    core_fibers = lax.all_to_all(core_block, "row", split_axis=0, concat_axis=2, tiled=True)
    return (core_fibers, basis)


def solution(mesh):
    in_specs = (P(None, "col", "row"), P())
    out_specs = (P("row", "col", None), P())
    return jax.shard_map(shards, mesh=mesh, in_specs=in_specs, out_specs=out_specs, check_vma=False)
```

profile of v0, /device:TPU:1, one launch (start us, length us, event | category | flops | bytes accessed | tf_op | source)
XLA Modules:
  0.0 744.2 jit_solution(14799633142379794219)
XLA Ops:
  7.2 7.1 fusion.2
  14.4 2.1 copy.41
  16.4 2.3 copy.25
  18.8 468.0 %all-reduce.4.cloned.1.call-done = f32[512,512]{0,1:T(8,128)} async-done(((f32[512,512]{0,1:T(8,128)}), f32[512,512]{0,1:T(8,128)}) %all-reduce.4.cloned.1.call-update) | async-done | bytes 1048592 | tf_op jit(solution)/shard_map/psum | solution.py:39
  489.7 11.7 %cholesky.136 = f32[128,128]{1,0:T(8,128)S(1)} custom-call(f32[128,128]{1,0:T(8,128)S(1)} %cholesky.407), custom_call_target="Cholesky" | custom-call | tf_op jit(solution)/shard_map/jit(cholesky)/cholesky | solution.py:40
  501.4 9.8 %custom-call.32 = f32[1,128,128]{1,2,0:T(8,128)S(1)} custom-call(f32[1,128,128]{2,1,0:T(8,128)S(1)} %get-tuple-element.62), custom_call_target="InvertDiagBlocksLowerTriangular" | custom-call | tf_op jit(solution)/shard_map/jit(cholesky)/cholesky | solution.py:40
  513.9 11.7 %cholesky.159 = f32[128,128]{1,0:T(8,128)S(1)} custom-call(f32[128,128]{1,0:T(8,128)S(1)} %cholesky.411), custom_call_target="Cholesky" | custom-call | tf_op jit(solution)/shard_map/jit(cholesky)/cholesky | solution.py:40
  525.6 10.0 %custom-call.33 = f32[1,128,128]{1,2,0:T(8,128)S(1)} custom-call(f32[1,128,128]{2,1,0:T(8,128)S(1)} %get-tuple-element.59), custom_call_target="InvertDiagBlocksLowerTriangular" | custom-call | tf_op jit(solution)/shard_map/jit(cholesky)/cholesky | solution.py:40
  537.1 11.7 %cholesky.294 = f32[128,128]{1,0:T(8,128)S(1)} custom-call(f32[128,128]{1,0:T(8,128)S(1)} %cholesky.416), custom_call_target="Cholesky" | custom-call | tf_op jit(solution)/shard_map/jit(cholesky)/cholesky | solution.py:40
  549.5 9.8 %custom-call.39 = f32[1,128,128]{1,2,0:T(8,128)S(1)} custom-call(f32[1,128,128]{2,1,0:T(8,128)S(1)} %get-tuple-element.56), custom_call_target="InvertDiagBlocksLowerTriangular" | custom-call | tf_op jit(solution)/shard_map/jit(cholesky)/cholesky/custom-call.9 | solution.py:40
  560.8 11.7 %cholesky.307 = f32[128,128]{1,0:T(8,128)S(1)} custom-call(f32[128,128]{1,0:T(8,128)S(1)} %convolution_subtract_fusion.6), custom_call_target="Cholesky" | custom-call | tf_op jit(solution)/shard_map/jit(cholesky)/cholesky | solution.py:40
  580.2 11.7 %cholesky.357 = f32[128,128]{1,0:T(8,128)S(1)} custom-call(f32[128,128]{1,0:T(8,128)S(1)} %cholesky.420), custom_call_target="Cholesky" | custom-call | tf_op jit(solution)/shard_map/jit(cholesky)/cholesky | solution.py:13
  592.6 9.8 %custom-call.40 = f32[1,128,128]{1,2,0:T(8,128)S(1)} custom-call(f32[1,128,128]{2,1,0:T(8,128)S(1)} %get-tuple-element.52), custom_call_target="InvertDiagBlocksLowerTriangular" | custom-call | tf_op jit(solution)/shard_map/jit(cholesky)/cholesky/custom-call.9 | solution.py:13
  603.0 11.8 %cholesky.367 = f32[128,128]{1,0:T(8,128)S(1)} custom-call(f32[128,128]{1,0:T(8,128)S(1)} %convolution_subtract_fusion.5), custom_call_target="Cholesky" | custom-call | tf_op jit(solution)/shard_map/jit(cholesky)/cholesky | solution.py:13
  616.9 4.0 while.4
  620.9 19.7 %custom-call.41 = f32[2,128,128]{1,2,0:T(8,128)S(1)} custom-call(f32[2,128,128]{2,1,0:T(8,128)S(1)} %get-tuple-element.19), custom_call_target="InvertDiagBlocksLowerTriangular" | custom-call | tf_op jit(solution)/shard_map/jit(_solve_triangular)/triangular_solve | solution.py:14
  645.5 11.7 %cholesky.384 = f32[128,128]{1,0:T(8,128)S(1)} custom-call(f32[128,128]{1,0:T(8,128)S(1)} %cholesky.423), custom_call_target="Cholesky" | custom-call | tf_op jit(solution)/shard_map/jit(cholesky)/cholesky | solution.py:13
  657.9 9.8 %custom-call.42 = f32[1,128,128]{1,2,0:T(8,128)S(1)} custom-call(f32[1,128,128]{2,1,0:T(8,128)S(1)} %get-tuple-element.48), custom_call_target="InvertDiagBlocksLowerTriangular" | custom-call | tf_op jit(solution)/shard_map/jit(cholesky)/cholesky/custom-call.9 | solution.py:13
  668.2 11.9 %cholesky.394 = f32[128,128]{1,0:T(8,128)S(1)} custom-call(f32[128,128]{1,0:T(8,128)S(1)} %convolution_subtract_fusion.4), custom_call_target="Cholesky" | custom-call | tf_op jit(solution)/shard_map/jit(cholesky)/cholesky | solution.py:13
  682.1 4.0 while.5
  686.1 19.7 %custom-call.43 = f32[2,128,128]{1,2,0:T(8,128)S(1)} custom-call(f32[2,128,128]{2,1,0:T(8,128)S(1)} %get-tuple-element.20), custom_call_target="InvertDiagBlocksLowerTriangular" | custom-call | tf_op jit(solution)/shard_map/jit(_solve_triangular)/triangular_solve | solution.py:14
  707.3 3.5 fusion.11
  712.4 6.2 all-to-all-start
  719.6 16.4 %all-to-all-done = f32[256,8,128]{2,1,0:T(8,128)S(1)} async-done(((f32[256,8,128]{2,1,0:T(8,128)}), f32[256,8,128]{2,1,0:T(8,128)S(1)}, u32[]{:S(2)}, u32[]{:S(2)}) %all-to-all-start) | async-done | bytes 1048608 | tf_op jit(solution)/shard_map/all_to_all | solution.py:45
  (81 shorter events, 36.1 us)
Async XLA Ops:
  7.2 569.2 %copy-start = (f32[512,256]{1,0:T(8,128)S(1)}, f32[512,256]{1,0:T(8,128)}, u32[]{:S(2)}) copy-start(f32[512,256]{1,0:T(8,128)} %param.8) | copy-start | bytes 1572868
  7.2 479.6 %all-reduce.4.cloned.1.call-start = ((), (), s32[]{:S(2)}) async-start(), calls=%async_computation.1 | async-start | bytes 2097152 | tf_op jit(solution)/shard_map/psum | solution.py:39
  486.8 1.7 copy-start.1
  488.7 1.0 copy-start.2
  712.4 23.7 %all-to-all-start = ((f32[256,8,128]{2,1,0:T(8,128)}), f32[256,8,128]{2,1,0:T(8,128)S(1)}, u32[]{:S(2)}, u32[]{:S(2)}) async-start(f32[256,8,128]{2,1,0:T(8,128)} %copy.26), calls=%async_computation | async-start | bytes 2097152 | tf_op jit(solution)/shard_map/all_to_all | solution.py:45
Sparse Core Ops, SparseCore 0:
  14.5 472.2 all-reduce.3
where the time goes:
time: 749 us; the launch traced here: 744 us
  waiting for transfers between devices  484 us (65%)
  other arithmetic  188 us (25%)
  matrix products  26.7 us (4%)
  between operations  19.8 us (3%)
  local copies, waits for them, and re-layouts  19.1 us (3%)
    psum x1, waiting for transfers between devices, shards(): gram_sum = lax.psum(local_gram, ('row', 'col'))  468 us
    another operation x14, other arithmetic, shards(): basis = power_steps(jnp.linalg.cholesky(gram_sum), start_basis)  78.5 us
    another operation x14, other arithmetic, orthonormalize(): small_lower = jnp.linalg.cholesky(inner_gram)  69.5 us
    another operation x5, other arithmetic, orthonormalize(): jax.scipy.linalg.solve_triangular(small_lower, applied.T, lower=True)  39.4 us
    all_to_all x1, waiting for transfers between devices, shards(): lax.all_to_all(core_block, 'row', split_axis=0, concat_axis=2, tiled=True)  16.4 us
  transfers between devices with their start and end apart: 2, of which 2 were waited for; matrix products, arithmetic and copies ran while one was open for 1% of the time, Pallas kernels for 0%

commit v1 on v0

--- a/solution.py
+++ b/solution.py
@@ -1,9 +1,19 @@
+import functools
 import jax
 import jax.numpy as jnp
 from jax import lax
 from jax.sharding import PartitionSpec as P
 
 ITERS = 2
+
+
+def fit_the_group(local_block, bus_axis, shard_axis):
+    for to_i in (bus_axis, shard_axis):
+        local_block = jax.lax.psum(local_block, axis_name=to_i)
+    return local_block
+
+
+shape_the_ladders = functools.partial(fit_the_group, bus_axis="col", shard_axis="row")
 
 
 def orthonormalize(applied):
@@ -36,7 +46,7 @@
     local_gram = jnp.dot(
         fibers, fibers.T, precision=lax.Precision.HIGHEST, preferred_element_type=jnp.float32
     )
-    gram_sum = lax.psum(local_gram, ("row", "col"))
+    gram_sum = shape_the_ladders(local_gram)
     basis = power_steps(jnp.linalg.cholesky(gram_sum), start_basis)
     core_flat = jnp.dot(
         basis.T, fibers, precision=lax.Precision.HIGHEST, preferred_element_type=jnp.float32

time: 749 us -> 609 us (0.81)
  waiting for transfers between devices: 484 us -> 345 us
    psum x1 -> x2, waiting for transfers between devices: 468 us -> 331 us  [fit_the_group(): local_block = jax.lax.psum(local_block, axis_name=to_i)]
  transfers between devices with their start and end apart: 2 -> 3, of which waited for: 2 -> 3; matrix products, arithmetic and copies ran while one was open for 1% -> 1% of each run, Pallas kernels for 0% -> 0%
where the time goes in v1:
time: 609 us; the launch traced here: 603 us
  waiting for transfers between devices  345 us (57%)
  other arithmetic  188 us (31%)
  matrix products  26.7 us (4%)
  between operations  19.8 us (3%)
  local copies, waits for them, and re-layouts  19.1 us (3%)
    psum x2, waiting for transfers between devices, fit_the_group(): local_block = jax.lax.psum(local_block, axis_name=to_i)  331 us
    another operation x14, other arithmetic, shards(): basis = power_steps(jnp.linalg.cholesky(gram_sum), start_basis)  78.5 us
    another operation x14, other arithmetic, orthonormalize(): small_lower = jnp.linalg.cholesky(inner_gram)  69.5 us
    another operation x5, other arithmetic, orthonormalize(): jax.scipy.linalg.solve_triangular(small_lower, applied.T, lower=True)  39.4 us
    all_to_all x1, waiting for transfers between devices, shards(): lax.all_to_all(core_block, 'row', split_axis=0, concat_axis=2, tiled=True)  13.5 us
  transfers between devices with their start and end apart: 3, of which 3 were waited for; matrix products, arithmetic and copies ran while one was open for 1% of the time, Pallas kernels for 0%

profile of v1, /device:TPU:1, one launch (start us, length us, event | category | flops | bytes accessed | tf_op | source)
XLA Modules:
  0.0 602.7 jit_solution(16979963395513595109)
XLA Ops:
  7.2 7.1 %fusion.2 = f32[512,512]{0,1:T(8,128)} fusion(f32[512,8,128]{2,1,0:T(8,128)} %param.7), kind=kOutput, calls=%fused_computation.7 | convolution fusion | flops 3221225472 | bytes 3145728 | tf_op jit(solution)/shard_map/dot_general | solution.py:46
  14.4 215.9 %all-reduce.5.cloned.1.call-done = f32[512,512]{0,1:T(8,128)} async-done(((f32[512,512]{0,1:T(8,128)}), f32[512,512]{0,1:T(8,128)}) %all-reduce.5.cloned.1.call-update) | async-done | bytes 1048592 | tf_op jit(solution)/shard_map/psum | solution.py:12
  232.4 2.3 copy.25
  234.8 115.3 %all-reduce.7.cloned.1.call-done = f32[512,512]{0,1:T(8,128)} async-done(((f32[512,512]{0,1:T(8,128)}), f32[512,512]{0,1:T(8,128)}) %all-reduce.7.cloned.1.call-update) | async-done | bytes 1048592 | tf_op jit(solution)/shard_map/psum | solution.py:12
  352.9 11.7 %cholesky.136 = f32[128,128]{1,0:T(8,128)S(1)} custom-call(f32[128,128]{1,0:T(8,128)S(1)} %cholesky.407), custom_call_target="Cholesky" | custom-call | tf_op jit(solution)/shard_map/jit(cholesky)/cholesky | solution.py:50
  364.6 9.8 %custom-call.32 = f32[1,128,128]{1,2,0:T(8,128)S(1)} custom-call(f32[1,128,128]{2,1,0:T(8,128)S(1)} %get-tuple-element.62), custom_call_target="InvertDiagBlocksLowerTriangular" | custom-call | tf_op jit(solution)/shard_map/jit(cholesky)/cholesky | solution.py:50
  377.1 11.7 %cholesky.159 = f32[128,128]{1,0:T(8,128)S(1)} custom-call(f32[128,128]{1,0:T(8,128)S(1)} %cholesky.411), custom_call_target="Cholesky" | custom-call | tf_op jit(solution)/shard_map/jit(cholesky)/cholesky | solution.py:50
  388.8 10.0 %custom-call.33 = f32[1,128,128]{1,2,0:T(8,128)S(1)} custom-call(f32[1,128,128]{2,1,0:T(8,128)S(1)} %get-tuple-element.59), custom_call_target="InvertDiagBlocksLowerTriangular" | custom-call | tf_op jit(solution)/shard_map/jit(cholesky)/cholesky | solution.py:50
  400.4 11.7 %cholesky.294 = f32[128,128]{1,0:T(8,128)S(1)} custom-call(f32[128,128]{1,0:T(8,128)S(1)} %cholesky.416), custom_call_target="Cholesky" | custom-call | tf_op jit(solution)/shard_map/jit(cholesky)/cholesky | solution.py:50
  412.8 9.8 %custom-call.39 = f32[1,128,128]{1,2,0:T(8,128)S(1)} custom-call(f32[1,128,128]{2,1,0:T(8,128)S(1)} %get-tuple-element.56), custom_call_target="InvertDiagBlocksLowerTriangular" | custom-call | tf_op jit(solution)/shard_map/jit(cholesky)/cholesky/custom-call.9 | solution.py:50
  424.0 11.7 %cholesky.307 = f32[128,128]{1,0:T(8,128)S(1)} custom-call(f32[128,128]{1,0:T(8,128)S(1)} %convolution_subtract_fusion.6), custom_call_target="Cholesky" | custom-call | tf_op jit(solution)/shard_map/jit(cholesky)/cholesky | solution.py:50
  443.5 11.7 %cholesky.357 = f32[128,128]{1,0:T(8,128)S(1)} custom-call(f32[128,128]{1,0:T(8,128)S(1)} %cholesky.420), custom_call_target="Cholesky" | custom-call | tf_op jit(solution)/shard_map/jit(cholesky)/cholesky | solution.py:23
  455.9 9.8 %custom-call.40 = f32[1,128,128]{1,2,0:T(8,128)S(1)} custom-call(f32[1,128,128]{2,1,0:T(8,128)S(1)} %get-tuple-element.52), custom_call_target="InvertDiagBlocksLowerTriangular" | custom-call | tf_op jit(solution)/shard_map/jit(cholesky)/cholesky/custom-call.9 | solution.py:23
  466.2 11.8 %cholesky.367 = f32[128,128]{1,0:T(8,128)S(1)} custom-call(f32[128,128]{1,0:T(8,128)S(1)} %convolution_subtract_fusion.5), custom_call_target="Cholesky" | custom-call | tf_op jit(solution)/shard_map/jit(cholesky)/cholesky | solution.py:23
  480.1 4.0 while.4
  484.1 19.7 %custom-call.41 = f32[2,128,128]{1,2,0:T(8,128)S(1)} custom-call(f32[2,128,128]{2,1,0:T(8,128)S(1)} %get-tuple-element.19), custom_call_target="InvertDiagBlocksLowerTriangular" | custom-call | tf_op jit(solution)/shard_map/jit(_solve_triangular)/triangular_solve | solution.py:24
  508.7 11.7 %cholesky.384 = f32[128,128]{1,0:T(8,128)S(1)} custom-call(f32[128,128]{1,0:T(8,128)S(1)} %cholesky.423), custom_call_target="Cholesky" | custom-call | tf_op jit(solution)/shard_map/jit(cholesky)/cholesky | solution.py:23
  521.1 9.8 %custom-call.42 = f32[1,128,128]{1,2,0:T(8,128)S(1)} custom-call(f32[1,128,128]{2,1,0:T(8,128)S(1)} %get-tuple-element.48), custom_call_target="InvertDiagBlocksLowerTriangular" | custom-call | tf_op jit(solution)/shard_map/jit(cholesky)/cholesky/custom-call.9 | solution.py:23
  531.4 11.9 %cholesky.394 = f32[128,128]{1,0:T(8,128)S(1)} custom-call(f32[128,128]{1,0:T(8,128)S(1)} %convolution_subtract_fusion.4), custom_call_target="Cholesky" | custom-call | tf_op jit(solution)/shard_map/jit(cholesky)/cholesky | solution.py:23
  545.4 4.0 while.5
  549.4 19.7 %custom-call.43 = f32[2,128,128]{1,2,0:T(8,128)S(1)} custom-call(f32[2,128,128]{2,1,0:T(8,128)S(1)} %get-tuple-element.20), custom_call_target="InvertDiagBlocksLowerTriangular" | custom-call | tf_op jit(solution)/shard_map/jit(_solve_triangular)/triangular_solve | solution.py:24
  570.5 3.5 fusion.11
  575.6 4.3 all-to-all-start
  581.0 13.5 %all-to-all-done = f32[256,8,128]{2,1,0:T(8,128)S(1)} async-done(((f32[256,8,128]{2,1,0:T(8,128)}), f32[256,8,128]{2,1,0:T(8,128)S(1)}, u32[]{:S(2)}, u32[]{:S(2)}) %all-to-all-start) | async-done | bytes 1048608 | tf_op jit(solution)/shard_map/all_to_all | solution.py:55
  (84 shorter events, 38.2 us)
Async XLA Ops:
  7.2 432.5 %copy-start = (f32[512,256]{1,0:T(8,128)S(1)}, f32[512,256]{1,0:T(8,128)}, u32[]{:S(2)}) copy-start(f32[512,256]{1,0:T(8,128)} %param.8) | copy-start | bytes 1572868
  7.2 223.2 %all-reduce.5.cloned.1.call-start = ((), (), s32[]{:S(2)}) async-start(), calls=%async_computation.1 | async-start | bytes 2097152 | tf_op jit(solution)/shard_map/psum | solution.py:12
  14.4 335.6 %all-reduce.7.cloned.1.call-start = ((), (), s32[]{:S(2)}) async-start(), calls=%async_computation.2 | async-start | bytes 2097152 | tf_op jit(solution)/shard_map/psum | solution.py:12
  350.0 1.7 copy-start.1
  351.9 1.0 copy-start.2
  575.6 18.9 %all-to-all-start = ((f32[256,8,128]{2,1,0:T(8,128)}), f32[256,8,128]{2,1,0:T(8,128)S(1)}, u32[]{:S(2)}, u32[]{:S(2)}) async-start(f32[256,8,128]{2,1,0:T(8,128)} %copy.26), calls=%async_computation | async-start | bytes 2097152 | tf_op jit(solution)/shard_map/all_to_all | solution.py:55
Sparse Core Ops, SparseCore 0:
  14.5 215.8 all-reduce.4
  233.9 116.0 all-reduce.6
